TPU v7x, 256 devices: a whole 4x4x8 slice. The times are simulated.
256 devices in a mesh: dp: 8 (over y, z_lo), expert: 32 (over z_hi, x, core).
Axes of the slice: x: 4, y: 4, z: 8 (z_hi: 4, z_lo: 2; z = z_hi * 2 + z_lo), core: 2. Of those that a mesh axis runs over, the one named last changes fastest.
Arguments:
- tokens: bfloat16 [32768, 2048], P(('dp', 'expert')), may hold values from -6 to 6
- cotangent: bfloat16 [32768, 2048], P(('dp', 'expert')), may hold values from -6 to 6
- routes: int32 [32768, 4], P(('dp', 'expert')), may hold values from 0 to 31, all different within a row; in each aligned block of 128 rows (0 to 127, 128 to 255, ...) at most 17 rows name the same one
- gates: float32 [32768, 4], P(('dp', 'expert')), may hold values from 0.1 to 1
- w_gate: bfloat16 [32, 2048, 768], P('expert'), may hold values from -0.125 to 0.125
- w_up: bfloat16 [32, 2048, 768], P('expert'), may hold values from -0.125 to 0.125
- w_down: bfloat16 [32, 768, 2048], P('expert'), may hold values from -0.21875 to 0.21875
Outputs:
- token_grad: bfloat16 [32768, 2048], P(('dp', 'expert'))
- gate_grad: float32 [32, 2048, 768], P('expert', None, 'dp')
- up_grad: float32 [32, 2048, 768], P('expert', None, 'dp')
- down_grad: float32 [32, 768, 2048], P('expert', 'dp')
Inputs may be any that keep to these rules, and one draw needn't show every extreme that they name: `routes`: each row names 4 different experts. Within the rows of one device no expert is named by more than 17 rows, a bound that some block reaches.
All inputs are finite; a program needn't handle non-finite values.
Results may differ from a plain program's by a relative error of at most 0.015.
Values may be sent and summed in bfloat16 or wider, within the bound.
A program may use at most 128 MiB of HBM per device.

v0:
```python
import jax
import jax.numpy as jnp
from jax import lax
from jax.sharding import PartitionSpec as P


def positions(routes_block, experts, capacity):
    flat = routes_block.reshape(-1)
    onehot = (flat[:, None] == jnp.arange(experts, dtype=jnp.int32)[None, :]).astype(jnp.int32)
    before = jnp.cumsum(onehot, axis=0) - onehot
    slot = jnp.sum(before * onehot, axis=1)
    return flat * capacity + slot


def placing(routes_block, gates_block, experts, capacity):
    dest = positions(routes_block, experts, capacity)
    hits = (jnp.arange(experts * capacity, dtype=jnp.int32)[:, None] == dest[None, :]).astype(
        jnp.float32
    )
    hits = hits.reshape(experts * capacity, routes_block.shape[0], routes_block.shape[1])
    return (jnp.sum(hits, axis=2), jnp.sum(hits * gates_block[None, :, :], axis=2))


def forward_part(rows_in, gate_mat, up_mat):
    pre_gate = jnp.dot(rows_in, gate_mat, preferred_element_type=jnp.float32)
    pre_up = jnp.dot(rows_in, up_mat, preferred_element_type=jnp.float32)
    sigma = jax.nn.sigmoid(pre_gate)
    act = pre_gate * sigma
    hidden = (act * pre_up).astype(jnp.bfloat16)
    return (pre_gate, pre_up, sigma, act, hidden)


def down_part_of(rows_grad, hidden, down_mat):
    d_hidden = lax.dot_general(
        rows_grad, down_mat, (((1,), (1,)), ((), ())), preferred_element_type=jnp.float32
    )
    down_part = lax.dot_general(
        hidden, rows_grad, (((0,), (0,)), ((), ())), preferred_element_type=jnp.float32
    )
    return (d_hidden, down_part.astype(jnp.bfloat16))


def inner_part(rows_in, state, d_hidden, gate_mat, up_mat):
    pre_gate, pre_up, sigma, act, hidden = state
    d_up = (d_hidden * act).astype(jnp.bfloat16)
    d_gate = (d_hidden * pre_up * sigma * (1.0 + pre_gate * (1.0 - sigma))).astype(jnp.bfloat16)
    gate_part = lax.dot_general(
        rows_in, d_gate, (((0,), (0,)), ((), ())), preferred_element_type=jnp.float32
    )
    up_part = lax.dot_general(
        rows_in, d_up, (((0,), (0,)), ((), ())), preferred_element_type=jnp.float32
    )
    back = lax.dot_general(
        d_gate, gate_mat, (((1,), (1,)), ((), ())), preferred_element_type=jnp.float32
    )
    back = back + lax.dot_general(
        d_up, up_mat, (((1,), (1,)), ((), ())), preferred_element_type=jnp.float32
    )
    return (back.astype(jnp.bfloat16), gate_part.astype(jnp.bfloat16), up_part.astype(jnp.bfloat16))


def body(tokens, cotangent, routes, gates, w_gate, w_up, w_down):
    ranks = lax.axis_size("expert")
    local = w_gate.shape[0]
    experts = ranks * local
    tok_rows, top = routes.shape
    width = tokens.shape[1]
    capacity = tok_rows * top // experts + 1
    plain, scaled = placing(routes, gates, experts, capacity)
    plain_half = plain.astype(jnp.bfloat16)
    slot_gate = jnp.sum(scaled, axis=1)
    sent_x = jnp.dot(plain_half, tokens, preferred_element_type=jnp.float32).astype(jnp.bfloat16)
    picked = jnp.dot(plain_half, cotangent, preferred_element_type=jnp.float32)
    sent_g = (picked * slot_gate[:, None]).astype(jnp.bfloat16)
    sent_x = sent_x.reshape(experts, capacity, width)
    sent_g = sent_g.reshape(experts, capacity, width)

    def arrange(got):
        return got.reshape(ranks, local, capacity, width)

    got_x, got_g = (
        lax.all_to_all(sent_x, "expert", split_axis=0, concat_axis=0, tiled=True),
        lax.all_to_all(sent_g, "expert", split_axis=0, concat_axis=0, tiled=True),
    )
    got_x = arrange(got_x)
    got_g = arrange(got_g)
    rows_x = got_x[:, 0].reshape(ranks * capacity, width)
    rows_g = got_g[:, 0].reshape(ranks * capacity, width)
    states = forward_part(rows_x, w_gate[0], w_up[0])
    downs = down_part_of(rows_g, states[4], w_down[0])
    down_parts = jnp.stack([downs[1]], axis=0)
    inners = inner_part(rows_x, states, downs[0], w_gate[0], w_up[0])
    backs = jnp.stack([inners[0].reshape(ranks, capacity, width)], axis=1)
    backs = backs.reshape(ranks * local, capacity, width)
    gate_parts = jnp.stack([inners[1]], axis=0)
    up_parts = jnp.stack([inners[2]], axis=0)
    gate_grad, up_grad, down_grad = (
        lax.psum_scatter(gate_parts, "dp", scatter_dimension=2, tiled=True).astype(jnp.float32),
        lax.psum_scatter(up_parts, "dp", scatter_dimension=2, tiled=True).astype(jnp.float32),
        lax.psum_scatter(down_parts, "dp", scatter_dimension=1, tiled=True).astype(jnp.float32),
    )
    returned = lax.all_to_all(backs, "expert", split_axis=0, concat_axis=0, tiled=True)
    returned = returned.reshape(experts * capacity, width)
    token_grad = lax.dot_general(
        plain_half, returned, (((0,), (0,)), ((), ())), preferred_element_type=jnp.float32
    ).astype(jnp.bfloat16)
    return (token_grad, gate_grad, up_grad, down_grad)


def solution(mesh):
    placed = (
        P(("dp", "expert"), None),
        P(("dp", "expert"), None),
        P(("dp", "expert"), None),
        P(("dp", "expert"), None),
        P("expert", None, None),
        P("expert", None, None),
        P("expert", None, None),
    )
    return jax.shard_map(
        body,
        mesh=mesh,
        in_specs=placed,
        out_specs=(
            P(("dp", "expert"), None),
            P("expert", None, "dp"),
            P("expert", None, "dp"),
            P("expert", "dp", None),
        ),
        check_vma=False,
    )
```

profile of v0, /device:TPU:1, one launch (start us, length us, event | category | flops | bytes accessed | tf_op | source)
XLA Modules:
  0.0 506.4 jit_solution(4718248298624074437)
XLA Ops:
  7.2 0.9 copy.39
  8.1 0.1 eq.44
  8.2 0.1 eq.40
  8.4 1.2 reduce-window.6
  9.5 0.2 slice_reduce_fusion
  9.8 0.1 fusion.19
  9.9 0.1 reduce_sum.34
  10.0 0.1 copy.42
  10.1 0.7 multiply_add_fusion
  10.8 1.0 select_reduce_fusion
  11.8 3.2 convolution_convert_fusion.3
  14.9 4.4 reshape.56
  19.3 12.6 %all-to-all-start.1 = ((bf16[32,17,2048]{2,1,0:T(8,128)(2,1)}), bf16[32,17,2048]{2,1,0:T(8,128)(2,1)}, u32[]{:S(2)}, u32[]{:S(2)}) async-start(bf16[32,17,2048]{2,1,0:T(8,128)(2,1)} %reshape.56), calls=%async_computation.1 | async-start | bytes 6291456 | tf_op jit(solution)/shard_map/all_to_all | solution.py:82
  31.9 3.1 multiply_convert_fusion
  35.1 4.3 reshape.55
  39.4 65.2 %all-to-all-done.1 = bf16[32,17,2048]{2,1,0:T(8,128)(2,1)} async-done(((bf16[32,17,2048]{2,1,0:T(8,128)(2,1)}), bf16[32,17,2048]{2,1,0:T(8,128)(2,1)}, u32[]{:S(2)}, u32[]{:S(2)}) %all-to-all-start.1) | async-done | bytes 2228256 | tf_op jit(solution)/shard_map/all_to_all | solution.py:82
  104.5 6.0 %all-to-all-start = ((bf16[32,17,2048]{2,1,0:T(8,128)(2,1)}), bf16[32,17,2048]{2,1,0:T(8,128)(2,1)}, u32[]{:S(2)}, u32[]{:S(2)}) async-start(bf16[32,17,2048]{2,1,0:T(8,128)(2,1)} %reshape.55), calls=%async_computation | async-start | bytes 6291456 | tf_op jit(solution)/shard_map/all_to_all | solution.py:83
  110.5 0.2 reduce-scatter.10.cloned.1.call-start
  110.8 4.4 reshape_squeeze_reshape.7
  115.2 4.9 fusion.2
  120.0 3.1 fusion.6
  123.1 44.5 %all-to-all-done = bf16[32,17,2048]{2,1,0:T(8,128)(2,1)} async-done(((bf16[32,17,2048]{2,1,0:T(8,128)(2,1)}), bf16[32,17,2048]{2,1,0:T(8,128)(2,1)}, u32[]{:S(2)}, u32[]{:S(2)}) %all-to-all-start) | async-done | bytes 2228256 | tf_op jit(solution)/shard_map/all_to_all | solution.py:83
  167.6 4.4 reshape_squeeze_reshape.6
  172.0 6.9 %multiply_convert_fusion.2 = (bf16[544,768]{1,0:T(8,128)(2,1)}, bf16[544,768]{1,0:T(8,128)(2,1)S(1)}) fusion(f32[544,768]{1,0:T(8,128)} %fusion.2, f32[544,768]{1,0:T(8,128)} %fusion.6, bf16[544,2048]{1,0:T(8,128)(2,1)} %reshape_squeeze_reshape.6, bf16[1,768,2048]{2,1,0:T(8,128)(2,1)} %param.13), kind=kOutput, calls=%fused_computation.23 | convolution fusion | flops 1716707328 | bytes 10387456 | tf_op jit(solution)/shard_map/dot_general | solution.py:34
  178.9 0.9 copy-done.5
  179.8 4.1 fusion.10
  183.9 15.7 %copy.45 = bf16[1,2048,768]{1,0,2:T(2,128)(2,1)} copy(bf16[1,2048,768]{2,1,0:T(8,128)(2,1)} %fusion.10) | data formatting | bytes 6291456
  199.6 6.4 %copy.56 = bf16[768,1,2048]{2,0,1:T(8,128)(2,1)} copy(bf16[768,1,2048]{2,1,0:T(2,128)(2,1)} %bitcast.70) | data formatting | bytes 6291456
  206.1 0.3 reduce-scatter.12.cloned.1.call-start
  206.4 6.1 %fusion.11 = bf16[1,2048,768]{2,1,0:T(8,128)(2,1)} fusion(bf16[544,2048]{1,0:T(8,128)(2,1)} %reshape_squeeze_reshape.7, bf16[544,768]{1,0:T(8,128)(2,1)} %get-tuple-element.26), kind=kOutput, calls=%fused_computation.19 | convolution fusion | flops 1712848896 | bytes 6209536 | tf_op jit(solution)/shard_map/dot_general | solution.py:50
  212.5 15.7 %copy.47 = bf16[1,2048,768]{1,0,2:T(2,128)(2,1)} copy(bf16[1,2048,768]{2,1,0:T(8,128)(2,1)} %fusion.11) | data formatting | bytes 6291456
  228.2 6.4 %copy.55 = bf16[768,1,2048]{2,0,1:T(8,128)(2,1)} copy(bf16[768,1,2048]{2,1,0:T(2,128)(2,1)} %bitcast.71) | data formatting | bytes 6291456
  234.7 7.0 %fusion.12 = bf16[1,768,2048]{2,1,0:T(8,128)(2,1)} fusion(bf16[544,2048]{1,0:T(8,128)(2,1)} %reshape_squeeze_reshape.6, f32[544,768]{1,0:T(8,128)} %fusion.6, f32[544,768]{1,0:T(8,128)} %fusion.2), kind=kOutput, calls=%fused_computation.20 | convolution fusion | flops 1715355648 | bytes 8716288 | tf_op jit(solution)/shard_map/dot_general | solution.py:37
  241.7 3.2 fusion
  245.0 3.3 add_convert_fusion
  248.3 4.4 reshape_stack_reshape.3
  252.7 117.0 %all_to_all.15 = bf16[32,17,2048]{2,1,0:T(8,128)(2,1)} all-to-all(bf16[32,17,2048]{2,1,0:T(8,128)(2,1)} %reshape_stack_reshape.3), channel_id=1, replica_groups=mesh['dp'=8,'expert'=32] {'expert'}, dimensions={0} | all-to-all | bytes 4456448 | tf_op jit(solution)/shard_map/all_to_all | solution.py:102
  369.6 4.3 reshape.57
  374.0 3.0 convolution_convert_fusion.4
  377.0 2.4 reshape_bitcast_fusion.1
  379.4 3.0 copy.46
  382.3 2.1 copy.43
  384.4 37.1 %reduce-scatter.12.cloned.1.call-done = bf16[96,2048]{1,0:T(8,128)(2,1)} async-done(((bf16[768,2048]{1,0:T(8,128)(2,1)}), bf16[96,2048]{1,0:T(8,128)(2,1)}) %reduce-scatter.12.cloned.1.call-update) | async-done | bytes 393232
  421.5 2.3 reshape_bitcast_fusion
  423.8 2.9 copy.48
  426.8 2.1 copy.44
  428.9 69.0 %reduce-scatter.8.cloned.1.call-done = bf16[1,96,2048]{2,1,0:T(8,128)(2,1)} async-done(((bf16[1,768,2048]{2,1,0:T(8,128)(2,1)}), bf16[1,96,2048]{2,1,0:T(8,128)(2,1)}) %reduce-scatter.8.cloned.1.call-update) | async-done | bytes 393232 | tf_op jit(solution)/shard_map/reduce_scatter | solution.py:100
  497.9 1.9 convert_element_type.69
  (21 shorter events, 0.2 us)
Async XLA Ops:
  7.2 108.0 %copy-start = (bf16[1,2048,768]{2,1,0:T(8,128)(2,1)S(1)}, bf16[1,2048,768]{2,1,0:T(8,128)(2,1)}, u32[]{:S(2)}) copy-start(bf16[1,2048,768]{2,1,0:T(8,128)(2,1)} %param.11) | copy-start | bytes 9437188
  19.3 85.3 %all-to-all-start.1 = ((bf16[32,17,2048]{2,1,0:T(8,128)(2,1)}), bf16[32,17,2048]{2,1,0:T(8,128)(2,1)}, u32[]{:S(2)}, u32[]{:S(2)}) async-start(bf16[32,17,2048]{2,1,0:T(8,128)(2,1)} %reshape.56), calls=%async_computation.1 | async-start | bytes 6291456 | tf_op jit(solution)/shard_map/all_to_all | solution.py:82
  104.5 63.1 %all-to-all-start = ((bf16[32,17,2048]{2,1,0:T(8,128)(2,1)}), bf16[32,17,2048]{2,1,0:T(8,128)(2,1)}, u32[]{:S(2)}, u32[]{:S(2)}) async-start(bf16[32,17,2048]{2,1,0:T(8,128)(2,1)} %reshape.55), calls=%async_computation | async-start | bytes 6291456 | tf_op jit(solution)/shard_map/all_to_all | solution.py:83
  110.5 266.5 %reduce-scatter.10.cloned.1.call-start = ((), (), s32[]{:S(2)}) async-start(), calls=%async_computation.7 | async-start | bytes 3538944
  115.2 4.9 copy-start.1
  115.2 4.9 copy-start.3
  172.0 7.8 %copy-start.2 = (bf16[544,2048]{1,0:T(8,128)(2,1)S(1)}, bf16[544,2048]{1,0:T(8,128)(2,1)}, u32[]{:S(2)}) copy-start(bf16[544,2048]{1,0:T(8,128)(2,1)} %reshape_squeeze_reshape.7) | copy-start | bytes 6684676
  178.9 0.9 copy-start.5
  206.1 215.4 %reduce-scatter.12.cloned.1.call-start = ((), (), s32[]{:S(2)}) async-start(), calls=%async_computation.8 | async-start | bytes 3538944
  234.6 263.3 %reduce-scatter.8.cloned.1.call-start = ((), (), s32[]{:S(2)}) async-start(), calls=%async_computation.6 | async-start | bytes 3538944 | tf_op jit(solution)/shard_map/reduce_scatter | solution.py:100
  241.7 3.3 copy-start.4
  241.7 3.3 copy-start.6
Sparse Core Ops, SparseCore 0:
  206.2 124.8 reduce-scatter.9
  333.6 87.8 reduce-scatter.11
  424.1 73.8 reduce-scatter.7
where the time goes:
time: 508 us; the launch traced here: 506 us
  waiting for transfers between devices  216 us (43%)
  blocking collectives  117 us (23%)
  local copies, waits for them, and re-layouts  87.8 us (17%)
  matrix products  48 us (9%)
  starting transfers between devices  19.1 us (4%)
  between operations  13.9 us (3%)
    all_to_all x1, blocking collectives, body(): lax.all_to_all(backs, 'expert', split_axis=0, concat_axis=0, tiled=True)  117 us
    reduce_scatter x1, waiting for transfers between devices, body(): lax.psum_scatter(down_parts, 'dp', scatter_dimension=1, tiled=True)  69 us
    all_to_all x1, waiting for transfers between devices, body(): lax.all_to_all(sent_x, 'expert', split_axis=0, concat_axis=0, tiled=True)  65.2 us
    unnamed x25, local copies, waits for them, and re-layouts  61 us
    all_to_all x1, waiting for transfers between devices, body(): lax.all_to_all(sent_g, 'expert', split_axis=0, concat_axis=0, tiled=True)  44.5 us
    unnamed x5, waiting for transfers between devices  37.1 us
    all_to_all x1, starting transfers between devices, body(): lax.all_to_all(sent_x, 'expert', split_axis=0, concat_axis=0, tiled=True)  12.6 us
  transfers between devices with their start and end apart: 5, of which 4 were waited for; matrix products, arithmetic and copies ran while one was open for 17% of the time, Pallas kernels for 0%

commit v1 on v0

v1 whole, which is shorter than its diff:
```python
import jax
import jax.numpy as jnp
from jax import lax
from jax.experimental import pallas as pl
from jax.experimental.pallas import tpu as pltpu
from jax.sharding import PartitionSpec as P

MESH = pl.DeviceIdType.MESH
F32 = jnp.float32
BF16 = jnp.bfloat16

D = 2048
H = 768
TOP = 4
TOK = 128
CAP = 17
NB = 4
NE = 8
PAD = 80
ROWS = NE * PAD
NQ = 4
C = D // NQ
HY = H // 4
HZ = HY // 2


def dot(a, b, dims=((1,), (0,))):
    return lax.dot_general(a, b, (dims, ((), ())), preferred_element_type=F32)


def kernel(
    info_in, tok_in, cot_in, wg_in, wu_in, wd_in,
    tg_out, down_out, gate_out, up_out,
    info, blk, sel, sgate, snd, rows, wg, wu, wd, pg, pu, dh,
    ht, dgt, dut, dg, du, brow, trow, pw, ra, rb, zs, zr_buf,
    in_sem, w_sem, is_sem, ir_sem, zs_sem, zr_sem, xs_sem, xr_sem,
    bs_sem, br_sem, ts_sem, tr_sem, as_sem, ar_sem, ds_sem, rb_sem, ms_sem, mr_sem,
):
    dp, ex = lax.axis_index("dp"), lax.axis_index("expert")
    y, zl = lax.div(dp, 2), lax.rem(dp, 2)
    zh, xc = lax.div(ex, NE), lax.rem(ex, NE)
    sign = 1 - 2 * zl
    zh_next, zh_prev = lax.rem(zh + sign + 4, 4), lax.rem(zh - sign + 4, 4)

    def dev(y_, zl_, zh_, xc_):
        return (y_ * 2 + zl_, zh_ * NE + xc_)

    up = dev(y, 0, lax.rem(zh + 1, 4), xc)
    down = dev(y, 1, lax.rem(zh + 3, 4), xc)
    ahead = dev(y, zl, zh_next, xc)
    prev_same = dev(y, zl, zh_prev, xc)
    prev_other = dev(y, 1 - zl, zh_prev, xc)
    y_up = dev(lax.rem(y + 1, 4), zl, zh, xc)
    y_down = dev(lax.rem(y + 3, 4), zl, zh, xc)
    mate = dev(y, 1 - zl, zh, xc)

    def copy(src, dst, send, recv, where):
        return pltpu.make_async_remote_copy(
            src_ref=src, dst_ref=dst, send_sem=send, recv_sem=recv,
            device_id=where, device_id_type=MESH)

    def landed(ref, sem):
        pltpu.make_async_copy(ref, ref, sem).wait()

    loads = []
    for q in range(2 * NQ):
        src = tok_in if q < NQ else cot_in
        loads.append(pltpu.make_async_copy(
            src.at[:, pl.ds(C * (q % NQ), C)], blk.at[q, 0], in_sem.at[q]))
    wloads = [pltpu.make_async_copy(a.at[0], b, w_sem.at[i])
              for i, (a, b) in enumerate(((wg_in, wg), (wu_in, wu), (wd_in, wd)))]
    for load in loads:
        load.start()
    for load in wloads:
        load.start()
    info[0] = info_in[...]

    barrier = pltpu.get_barrier_semaphore()
    for where in (ahead, prev_same, prev_other, y_up, y_down, mate):
        pl.semaphore_signal(barrier, inc=1, device_id=where, device_id_type=MESH)

    def greet(i, carry):
        peer = lax.rem(xc + i, NE)
        pl.semaphore_signal(barrier, inc=1, device_id=dev(y, zl, zh, peer), device_id_type=MESH)
        return carry

    lax.fori_loop(1, NE, greet, 0)
    pl.semaphore_wait(barrier, 6 + NE - 1)

    def z_copy(ref, i, send, recv):
        if i == 0:
            return copy(ref.at[0], ref.at[1 + zl], send.at[0], recv.at[zl], up)
        if i == 1:
            return copy(ref.at[0], ref.at[2 - zl], send.at[1], recv.at[1 - zl], down)
        return copy(ref.at[2], ref.at[3], send.at[2], recv.at[2], ahead)

    def block_copy(q, i):
        return z_copy(blk.at[q], i, zs_sem.at[q], zr_sem.at[q])

    icopies = [z_copy(info, i, is_sem, ir_sem) for i in range(3)]
    icopies[0].start()
    icopies[1].start()
    for load in loads:
        load.wait()

    def send_own(q):
        block_copy(q, 0).start()
        block_copy(q, 1).start()

    for q in range(2):
        send_own(q)

    landed(info.at[2], ir_sem.at[1])
    icopies[2].start()
    landed(info.at[1], ir_sem.at[0])
    landed(info.at[3], ir_sem.at[2])

    before_mask = (lax.broadcasted_iota(jnp.int32, (TOK, TOK), 0)
                   < lax.broadcasted_iota(jnp.int32, (TOK, TOK), 1)).astype(F32).astype(BF16)
    expert = (lax.broadcasted_iota(jnp.int32, (NE, TOK), 0) + NE * zh).astype(F32)
    slot = lax.broadcasted_iota(jnp.int32, (PAD, TOK), 0).astype(F32)
    scales = [jnp.zeros((PAD, 1), F32) for _ in range(NE)]
    for b in range(NB):
        chosen = jnp.zeros((NE, TOK), F32)
        weight = jnp.zeros((NE, TOK), F32)
        for k in range(TOP):
            hit = info[b, k:k + 1, :] == expert
            chosen = chosen + jnp.where(hit, 1.0, 0.0)
            weight = weight + jnp.where(hit, info[b, TOP + k:TOP + k + 1, :], 0.0)
        place = dot(chosen.astype(BF16), before_mask) + float(CAP * b)
        place = jnp.where(chosen > 0.0, place, -1.0)
        for j in range(NE):
            mine = jnp.where(slot == place[j:j + 1, :], 1.0, 0.0)
            sel[PAD * j:PAD * (j + 1), TOK * b:TOK * (b + 1)] = mine.astype(BF16)
            scales[j] = scales[j] + jnp.sum(mine * weight[j:j + 1, :], axis=1, keepdims=True)
    for j in range(NE):
        sgate[PAD * j:PAD * (j + 1), :] = jnp.broadcast_to(scales[j], (PAD, 128))

    pg[...] = jnp.zeros_like(pg)
    pu[...] = jnp.zeros_like(pu)
    dh[...] = jnp.zeros_like(dh)

    def spread(src, dst, send, recv):
        def one(i, carry):
            peer = lax.rem(xc + i, NE)
            copy(src.at[peer], dst.at[xc], send, recv, dev(y, zl, zh, peer)).start()
            return carry

        lax.fori_loop(1, NE, one, 0)

    def pick(q):
        block = blk.at[q]

        def part(n, carry):
            cols = pl.ds(pl.multiple_of(n * 256, 256), 256)
            got = dot(sel[...], block[:, :, cols].reshape(NB * TOK, 256))
            got = got * jnp.where(q >= NQ, sgate[:, 0:1], 1.0)
            snd[q, :, :, cols] = got.astype(BF16).reshape(NE, PAD, 256)
            return carry

        lax.fori_loop(0, C // 256, part, 0)
        spread(snd.at[q], rows.at[q], xs_sem.at[q], xr_sem.at[q])
        rows[q, xc] = snd[q, xc]

    def chunk_of(ref, q):
        return ref[q].reshape(ROWS, C)

    def forward(q):
        span = pl.ds(pl.multiple_of(q * C, C), C)

        def part(n, carry):
            cols = pl.ds(pl.multiple_of(n * 256, 256), 256)
            pg[:, cols] += dot(chunk_of(rows, q), wg[span, cols])
            pu[:, cols] += dot(chunk_of(rows, q), wu[span, cols])
            return carry

        lax.fori_loop(0, H // 256, part, 0)

    def activate():
        def part(n, carry):
            cols = pl.ds(pl.multiple_of(n * 128, 128), 128)
            pre, mul = pg[:, cols], pu[:, cols]
            sigma = jax.nn.sigmoid(pre)
            act = pre * sigma
            ht[cols, :] = jnp.transpose(act * mul).astype(BF16)
            pg[:, cols] = act
            pu[:, cols] = mul * sigma * (1.0 + pre * (1.0 - sigma))
            return carry

        lax.fori_loop(0, H // 128, part, 0)

    def backward(q):
        span = pl.ds(pl.multiple_of((q - NQ) * C, C), C)

        def part(n, carry):
            cols = pl.ds(pl.multiple_of(n * 256, 256), 256)
            dh[:, cols] += dot(chunk_of(rows, q), wd[cols, span], ((1,), (1,)))
            return carry

        lax.fori_loop(0, H // 256, part, 0)

    def stage(s, carry):
        @pl.when(s + 2 < 2 * NQ)
        def _():
            send_own(s + 2)

        @pl.when(s < 2 * NQ)
        def _():
            landed(blk.at[s, 2], zr_sem.at[s, 1])
            block_copy(s, 2).start()
            landed(blk.at[s, 1], zr_sem.at[s, 0])

        @pl.when((s >= 1) & (s < 2 * NQ + 1))
        def _():
            landed(blk.at[s - 1, 3], zr_sem.at[s - 1, 2])
            pick(s - 1)

        @pl.when(s >= 2)
        def _():
            q = s - 2
            landed(rows.at[q, pl.ds(0, NE - 1)], xr_sem.at[q])

            @pl.when(q < NQ)
            def _():
                forward(q)

            @pl.when(q == NQ - 1)
            def _():
                activate()

            @pl.when(q >= NQ)
            def _():
                backward(q)

        return carry

    for load in wloads:
        load.wait()
    lax.fori_loop(0, 2 * NQ + 2, stage, 0)

    def derive(n, carry):
        cols = pl.ds(pl.multiple_of(n * 128, 128), 128)
        grad = dh[:, cols]
        d_up = grad * pg[:, cols]
        d_gate = grad * pu[:, cols]
        du[:, cols] = d_up.astype(BF16)
        dg[:, cols] = d_gate.astype(BF16)
        dut[cols, :] = jnp.transpose(d_up).astype(BF16)
        dgt[cols, :] = jnp.transpose(d_gate).astype(BF16)
        return carry

    lax.fori_loop(0, H // 128, derive, 0)

    lefts = (ht, dgt, dut)
    firsts = (NQ, 0, 0)

    def partial(w, start, size, q):
        at = pl.ds(pl.multiple_of(start, 16), size)
        return dot(lefts[w][at, :], chunk_of(rows, firsts[w] + q))

    def partials(w, r):
        start = HY * lax.rem(y + r + 1, 4)

        def part(q, carry):
            cols = pl.ds(pl.multiple_of(q * C, C), C)
            pw[w, r, :, :, cols] = partial(w, start, HY, q).astype(BF16).reshape(2, HZ, C)
            return carry

        lax.fori_loop(0, NQ, part, 0)

    def far_copy(w, i):
        return copy(pw.at[w, 1, i], ra.at[w, i], as_sem.at[w, i], ar_sem.at[w, i],
                    y_down if i else y_up)

    def ring_copy(w, i, h):
        return copy(pw.at[w, 2 * i, h], rb.at[w, i, h], ds_sem.at[w, i, h], rb_sem.at[w, i, h],
                    y_down if i else y_up)

    for w in range(3):
        partials(w, 1)
        for i in range(2):
            far_copy(w, i).start()

    def sent(q, carry):
        landed(snd.at[q, pl.ds(0, NE - 1)], xs_sem.at[q])
        for i in range(3):
            block_copy(q, i).wait_send()
        return carry

    lax.fori_loop(0, 2 * NQ, sent, 0)
    for c in icopies:
        c.wait_send()

    def back(q, carry):
        def part(n, carry):
            at = pl.ds(pl.multiple_of(q * C + n * 256, 256), 256)
            cols = pl.ds(pl.multiple_of(n * 256, 256), 256)
            got = dot(dg[...], wg[at, :], ((1,), (1,))) + dot(du[...], wu[at, :], ((1,), (1,)))
            snd[q, :, :, cols] = got.astype(BF16).reshape(NE, PAD, 256)
            return carry

        lax.fori_loop(0, C // 256, part, 0)
        spread(snd.at[q], brow.at[q], bs_sem.at[q], br_sem.at[q])
        brow[q, xc] = snd[q, xc]
        return carry

    lax.fori_loop(0, NQ, back, 0)

    for w in range(3):
        partials(w, 0)
        partials(w, 2)
        for i in range(2):
            ring_copy(w, i, 1 - i).start()

    def t_copy(q, b):
        at = 2 if b == 3 else zl
        return copy(blk.at[q, b], trow.at[q, at], ts_sem.at[q, b - 1], tr_sem.at[q, at],
                    prev_other if b == 2 else prev_same)

    def combine(q):
        landed(brow.at[q, pl.ds(0, NE - 1)], br_sem.at[q])
        for b in (3, 1, 2, 0):
            got = dot(sel[:, TOK * b:TOK * (b + 1)], chunk_of(brow, q), ((0,), (0,)))
            if b:
                blk[q, b] = got.astype(BF16)
            else:
                pg[pl.ds(pl.multiple_of(q * TOK, TOK), TOK), 0:C] = got
            if b in (1, 3):
                t_copy(q, b).start()

    def pass_on(q):
        landed(trow.at[q, 2], tr_sem.at[q, 2])
        blk[q, 2] = (blk[q, 2].astype(F32) + trow[q, 2].astype(F32)).astype(BF16)
        t_copy(q, 2).start()

    def relay(w):
        for i in range(2):
            far_copy(w, i).wait_send()
            landed(ra.at[w, i], ar_sem.at[w, i])
            pw[w, 2 * i, i] = (pw[w, 2 * i, i].astype(F32) + ra[w, i].astype(F32)).astype(BF16)
            ring_copy(w, i, i).start()

    def return_step(q, carry):
        @pl.when(q < NQ)
        def _():
            combine(q)

        @pl.when(q >= 1)
        def _():
            pass_on(q - 1)

        @pl.when(q < 3)
        def _():
            relay(q)

        return carry

    lax.fori_loop(0, NQ + 1, return_step, 0)

    def finish_tokens(q, carry):
        landed(trow.at[q, 0], tr_sem.at[q, 0])
        landed(trow.at[q, 1], tr_sem.at[q, 1])
        cols = pl.ds(pl.multiple_of(q * C, C), C)
        total = pg[pl.ds(pl.multiple_of(q * TOK, TOK), TOK), 0:C]
        total = total + trow[q, 0].astype(F32) + trow[q, 1].astype(F32)
        tg_out[:, cols] = total.astype(BF16)
        for b in (1, 2, 3):
            t_copy(q, b).wait_send()
        return carry

    lax.fori_loop(0, NQ, finish_tokens, 0)

    outs = (down_out, gate_out, up_out)

    def mate_copy(w):
        return copy(zs.at[w], zr_buf.at[w], ms_sem.at[w], mr_sem.at[w], mate)

    def summed(w, half, q):
        cols = pl.ds(pl.multiple_of(q * C, C), C)
        own = partial(w, HY * y + HZ * half, HZ, q)
        return own + rb[w, 0, half, :, cols].astype(F32) + rb[w, 1, half, :, cols].astype(F32)

    for w in range(3):
        for i in range(2):
            for h in range(2):
                landed(rb.at[w, i, h], rb_sem.at[w, i, h])

        def give(q, carry):
            cols = pl.ds(pl.multiple_of(q * C, C), C)
            zs[w, :, cols] = summed(w, 1 - zl, q).astype(BF16)
            return carry

        lax.fori_loop(0, NQ, give, 0)
        mate_copy(w).start()

        def keep(q, carry):
            cols = pl.ds(pl.multiple_of(q * C, C), C)
            outs[w][:, cols] = summed(w, zl, q)
            return carry

        lax.fori_loop(0, NQ, keep, 0)

    for w in range(3):
        landed(zr_buf.at[w], mr_sem.at[w])
        outs[w][...] += zr_buf[w].astype(F32)
    for w in range(3):
        mate_copy(w).wait_send()
        for i in range(2):
            for h in range(2):
                ring_copy(w, i, h).wait_send()

    def back_sent(q, carry):
        landed(snd.at[q, pl.ds(0, NE - 1)], bs_sem.at[q])
        return carry

    lax.fori_loop(0, NQ, back_sent, 0)


def body(tokens, cotangent, routes, gates, w_gate, w_up, w_down):
    info = jnp.concatenate([routes.T.astype(F32), gates.T], axis=0)
    hbm = pl.BlockSpec(memory_space=pl.ANY)
    vmem = pl.BlockSpec(memory_space=pltpu.VMEM)
    V, S = pltpu.VMEM, pltpu.SemaphoreType.DMA
    token_grad, down, gate, up = pl.pallas_call(
        kernel,
        out_shape=(
            jax.ShapeDtypeStruct((TOK, D), BF16),
            jax.ShapeDtypeStruct((HZ, D), F32),
            jax.ShapeDtypeStruct((HZ, D), F32),
            jax.ShapeDtypeStruct((HZ, D), F32),
        ),
        in_specs=[vmem, hbm, hbm, hbm, hbm, hbm],
        out_specs=(vmem, vmem, vmem, vmem),
        scratch_shapes=[
            V((NB, 2 * TOP, TOK), F32),
            V((2 * NQ, NB, TOK, C), BF16),
            V((ROWS, NB * TOK), BF16),
            V((ROWS, 128), F32),
            V((2 * NQ, NE, PAD, C), BF16),
            V((2 * NQ, NE, PAD, C), BF16),
            V((D, H), BF16), V((D, H), BF16), V((H, D), BF16),
            V((ROWS, H), F32), V((ROWS, H), F32), V((ROWS, H), F32),
            V((H, ROWS), BF16), V((H, ROWS), BF16), V((H, ROWS), BF16),
            V((ROWS, H), BF16), V((ROWS, H), BF16),
            V((NQ, NE, PAD, C), BF16),
            V((NQ, 3, TOK, C), BF16),
            V((3, 3, 2, HZ, D), BF16),
            V((3, 2, HZ, D), BF16),
            V((3, 2, 2, HZ, D), BF16),
            V((3, HZ, D), BF16), V((3, HZ, D), BF16),
            S((2 * NQ,)), S((3,)), S((3,)), S((3,)),
            S((2 * NQ, 3)), S((2 * NQ, 3)), S((2 * NQ,)), S((2 * NQ,)),
            S((NQ,)), S((NQ,)), S((NQ, 3)), S((NQ, 3)),
            S((3, 2)), S((3, 2)), S((3, 2, 2)), S((3, 2, 2)), S((3,)), S((3,)),
        ],
        compiler_params=pltpu.CompilerParams(
            collective_id=0, has_side_effects=True, vmem_limit_bytes=62 * 1024 * 1024),
        cost_estimate=pl.CostEstimate(
            flops=8 * 2 * ROWS * D * H, bytes_accessed=16 * 1024 * 1024, transcendentals=ROWS * H),
    )(info, tokens, cotangent, w_gate, w_up, w_down)
    return token_grad, gate.T[None], up.T[None], down[None]


def solution(mesh):
    rows = P(("dp", "expert"), None)
    return jax.shard_map(
        body,
        mesh=mesh,
        in_specs=(rows, rows, rows, rows) + (P("expert", None, None),) * 3,
        out_specs=(rows, P("expert", None, "dp"), P("expert", None, "dp"), P("expert", "dp", None)),
        check_vma=False,
    )
```

time: 508 us -> 206 us (0.41)
  waiting for transfers between devices: 216 us -> 0 us
  Pallas kernels: 0 us -> 197 us
  blocking collectives: 117 us -> 0 us
  local copies, waits for them, and re-layouts: 87.8 us -> 5.83 us
  matrix products: 48 us -> 0 us
  starting transfers between devices: 19.1 us -> 0 us
  between operations: 13.9 us -> 0.66 us
    pallas_call x0 -> x1, Pallas kernels: none -> 197 us  [body(): pl.pallas_call(kernel, out_shape=(jax.ShapeDtypeStruct((TOK, D), BF16), j...]
    all_to_all x1 -> x0, blocking collectives: 117 us -> none  [body(): lax.all_to_all(backs, 'expert', split_axis=0, concat_axis=0, tiled=True)]
    all_to_all x2 -> x0, waiting for transfers between devices: 110 us -> none  [the longest x1 65.2 us: body(): lax.all_to_all(sent_x, 'expert', split_axis=0, concat_axis=0, tiled=True)]
    reduce_scatter x1 -> x0, waiting for transfers between devices: 69 us -> none  [body(): lax.psum_scatter(down_parts, 'dp', scatter_dimension=1, tiled=True)]
    unnamed x25 -> x8, local copies, waits for them, and re-layouts: 61 us -> 5.83 us
    dot_general x11 -> x0, matrix products: 48 us -> none  [the longest x1 7 us: down_part_of(): lax.dot_general(hidden, rows_grad, (((0,), (0,)), ((), ())), preferred_el...]
    unnamed x5 -> x0, waiting for transfers between devices: 37.1 us -> none
    all_to_all x2 -> x0, starting transfers between devices: 18.6 us -> none  [the longest x1 12.6 us: body(): lax.all_to_all(sent_x, 'expert', split_axis=0, concat_axis=0, tiled=True)]
  transfers between devices with their start and end apart: 5 -> 0, of which waited for: 4 -> 0; matrix products, arithmetic and copies ran while one was open for 17% -> 0% of each run, Pallas kernels for 0% -> 0%
where the time goes in v1:
time: 206 us
  Pallas kernels  197 us (96%)
  local copies, waits for them, and re-layouts  5.83 us (3%)
    pallas_call x1, Pallas kernels, body(): pl.pallas_call(kernel, out_shape=(jax.ShapeDtypeStruct((TOK, D), BF16), j...  197 us
    unnamed x8, local copies, waits for them, and re-layouts  5.83 us

profile of v1, /device:TPU:1, one launch (start us, length us, event | category | flops | bytes accessed | tf_op | source)
XLA Modules:
  0.0 205.9 jit_solution(14708986000192433182)
XLA Ops:
  0.6 0.7 convert_bitcast_fusion
  1.3 1.3 pad_maximum_fusion.info_in
  2.6 197.4 %shard_map.102 = (bf16[128,2048]{1,0:T(8,128)(2,1)}, f32[96,2048]{1,0:T(8,128)}, f32[96,2048]{1,0:T(8,128)}, f32[96,2048]{1,0:T(8,128)}) custom-call(f32[8,128]{1,0:T(8,128)} %pad_maximum_fusion.info_in, bf16[128,2048]{1,0:T(8,128)(2,1)} %tok_in.1, bf16[128,2048]{1,0:T(8,128)(2,1)} %cot_in.1, bf16[1,2048,768]{2,1,0:T(8,128)(2,1)} %wg_in.1, ...), custom_call_target="tpu_custom_call" | custom-call | flops 16106127360 | bytes 16777216 | tf_op jit(solution)/shard_map/pallas_call | solution.py:424
  200.0 0.0 copy-start.1
  200.0 0.0 copy-start
  200.0 2.0 copy.15
  202.0 2.1 %copy.16 = f32[1,2048,96]{1,2,0:T(8,128)} copy(f32[1,2048,96]{1,2,0:T(8,128)} %bitcast.12) | data formatting | bytes 1572864
  204.1 0.0 copy-done.1
  204.1 0.9 copy.17
  205.0 0.0 copy-done
  205.0 0.9 copy.18
Async XLA Ops:
  200.0 4.1 %copy-start.1 = (f32[96,2048]{1,0:T(8,128)S(1)}, f32[96,2048]{1,0:T(8,128)}, u32[]{:S(2)}) copy-start(f32[96,2048]{1,0:T(8,128)} %get-tuple-element.10) | copy-start | bytes 2359300
  200.0 5.0 %copy-start = (f32[96,2048]{1,0:T(8,128)S(1)}, f32[96,2048]{1,0:T(8,128)}, u32[]{:S(2)}) copy-start(f32[96,2048]{1,0:T(8,128)} %get-tuple-element.11) | copy-start | bytes 2359300

commit v2 on v1

v2 whole, which is shorter than its diff:
```python
import jax
import jax.numpy as jnp
from jax import lax
from jax.experimental import pallas as pl
from jax.experimental.pallas import tpu as pltpu
from jax.sharding import PartitionSpec as P

MESH = pl.DeviceIdType.MESH
F32 = jnp.float32
BF16 = jnp.bfloat16

D = 2048
H = 768
TOP = 4
TOK = 128
CAP = 17
NB = 4
NE = 8
PAD = 80
ROWS = NE * PAD
NQ = 8
C = D // NQ
AHEAD = 4
NG = 4
GC = D // NG
NU = 3 * NG
HY = H // 4
HZ = HY // 2


def dot(a, b, dims=((1,), (0,))):
    return lax.dot_general(a, b, (dims, ((), ())), preferred_element_type=F32)


def kernel(
    routes_in, gates_in, tok_in, cot_in, wg_in, wu_in, wd_in,
    tg_out, down_out, gate_out, up_out,
    info, blk, sel, selt, sgate, snd, rows, wg, wu, wd, pg, pu, dh,
    ht, dgt, dut, dg, du, brow, trow, pw, ra, rb, given,
    in_sem, w_sem, is_sem, ir_sem, zs_sem, zr_sem, xs_sem, xr_sem,
    bs_sem, br_sem, ts_sem, tr_sem, ys_sem, ya_sem, yb_sem, ms_sem, mr_sem,
):
    dp, ex = lax.axis_index("dp"), lax.axis_index("expert")
    y, zl = lax.div(dp, 2), lax.rem(dp, 2)
    zh, xc = lax.div(ex, NE), lax.rem(ex, NE)
    sign = 1 - 2 * zl
    zh_next, zh_prev = lax.rem(zh + sign + 4, 4), lax.rem(zh - sign + 4, 4)
    y1, y2, y3 = lax.rem(y + 1, 4), lax.rem(y + 2, 4), lax.rem(y + 3, 4)

    def dev(y_, zl_, zh_, xc_):
        return (y_ * 2 + zl_, zh_ * NE + xc_)

    up = dev(y, 0, lax.rem(zh + 1, 4), xc)
    down = dev(y, 1, lax.rem(zh + 3, 4), xc)
    ahead = dev(y, zl, zh_next, xc)
    prev_same = dev(y, zl, zh_prev, xc)
    prev_other = dev(y, 1 - zl, zh_prev, xc)
    y_up = dev(y1, zl, zh, xc)
    y_down = dev(y3, zl, zh, xc)
    mate = dev(y, 1 - zl, zh, xc)

    def copy(src, dst, send, recv, where):
        return pltpu.make_async_remote_copy(
            src_ref=src, dst_ref=dst, send_sem=send, recv_sem=recv,
            device_id=where, device_id_type=MESH)

    def landed(ref, sem):
        pltpu.make_async_copy(ref, ref, sem).wait()

    def span(n, size):
        return pl.ds(pl.multiple_of(n * size, size), size)

    loads = []
    for q in range(2 * NQ):
        src = tok_in if q < NQ else cot_in
        loads.append(pltpu.make_async_copy(
            src.at[:, pl.ds(C * (q % NQ), C)], blk.at[q, 0], in_sem.at[q]))
    wloads = [pltpu.make_async_copy(a.at[0], b, w_sem.at[i])
              for i, (a, b) in enumerate(((wg_in, wg), (wu_in, wu), (wd_in, wd)))]
    barrier = pltpu.get_barrier_semaphore()
    for where in (ahead, prev_same, prev_other, y_up, y_down, mate):
        pl.semaphore_signal(barrier, inc=1, device_id=where, device_id_type=MESH)

    def greet(i, carry):
        peer = lax.rem(xc + i, NE)
        pl.semaphore_signal(barrier, inc=1, device_id=dev(y, zl, zh, peer), device_id_type=MESH)
        return carry

    lax.fori_loop(1, NE, greet, 0)
    for load in loads:
        load.start()
    for load in wloads:
        load.start()
    info[0, 0:TOP] = routes_in[...].astype(F32)
    info[0, TOP:2 * TOP] = gates_in[...]
    for load in loads:
        load.wait()
    pl.semaphore_wait(barrier, 6 + NE - 1)

    def z_copy(ref, i, send, recv):
        if i == 0:
            return copy(ref.at[0], ref.at[1 + zl], send, recv.at[zl], up)
        if i == 1:
            return copy(ref.at[0], ref.at[2 - zl], send, recv.at[1 - zl], down)
        return copy(ref.at[2], ref.at[3], send, recv.at[2], ahead)

    def block_copy(q, i):
        return z_copy(blk.at[q], i, zs_sem.at[0], zr_sem.at[q])

    def info_copy(i):
        return z_copy(info, i, is_sem.at[0], ir_sem)

    info_copy(0).start()
    info_copy(1).start()

    def send_own(q):
        block_copy(q, 0).start()
        block_copy(q, 1).start()

    for q in range(AHEAD):
        send_own(q)
    landed(info.at[2], ir_sem.at[1])
    info_copy(2).start()
    pg[...] = jnp.zeros_like(pg)
    pu[...] = jnp.zeros_like(pu)
    dh[...] = jnp.zeros_like(dh)

    def build():
        landed(info.at[1], ir_sem.at[0])
        landed(info.at[3], ir_sem.at[2])
        before_mask = (lax.broadcasted_iota(jnp.int32, (TOK, TOK), 0)
                       < lax.broadcasted_iota(jnp.int32, (TOK, TOK), 1)).astype(F32).astype(BF16)
        expert = (lax.broadcasted_iota(jnp.int32, (NE, TOK), 0) + NE * zh).astype(F32)
        slot = lax.broadcasted_iota(jnp.int32, (PAD, TOK), 0).astype(F32)
        scales = [jnp.zeros((PAD, 1), F32) for _ in range(NE)]
        for b in range(NB):
            chosen = jnp.zeros((NE, TOK), F32)
            weight = jnp.zeros((NE, TOK), F32)
            for k in range(TOP):
                hit = info[b, k:k + 1, :] == expert
                chosen = chosen + jnp.where(hit, 1.0, 0.0)
                weight = weight + jnp.where(hit, info[b, TOP + k:TOP + k + 1, :], 0.0)
            place = dot(chosen.astype(BF16), before_mask) + float(CAP * b)
            place = jnp.where(chosen > 0.0, place, -1.0)
            for j in range(NE):
                mine = jnp.where(slot == place[j:j + 1, :], 1.0, 0.0)
                sel[PAD * j:PAD * (j + 1), TOK * b:TOK * (b + 1)] = mine.astype(BF16)
                scales[j] = scales[j] + jnp.sum(mine * weight[j:j + 1, :], axis=1, keepdims=True)
        for j in range(NE):
            sgate[PAD * j:PAD * (j + 1), :] = jnp.broadcast_to(scales[j], (PAD, 128))

    def flip():
        for b in range(NB):
            at = slice(TOK * b, TOK * (b + 1))
            selt[at, :] = jnp.transpose(sel[:, at].astype(F32)).astype(BF16)

    def spread(src, dst, send, recv):
        def one(i, carry):
            peer = lax.rem(xc + i, NE)
            copy(src.at[peer], dst.at[xc], send, recv, dev(y, zl, zh, peer)).start()
            return carry

        lax.fori_loop(1, NE, one, 0)

    def pick(q):
        got = dot(sel[...], blk[q].reshape(NB * TOK, C))
        got = got * jnp.where(q >= NQ, sgate[:, 0:1], 1.0)
        snd[q] = got.astype(BF16).reshape(NE, PAD, C)
        spread(snd.at[q], rows.at[q], xs_sem.at[0], xr_sem.at[q])
        rows[q, xc] = snd[q, xc]

    def chunk_of(ref, q):
        return ref[q].reshape(ROWS, C)

    def forward(q):
        def part(n, carry):
            cols = span(n, 256)
            pg[:, cols] += dot(chunk_of(rows, q), wg[span(q, C), cols])
            pu[:, cols] += dot(chunk_of(rows, q), wu[span(q, C), cols])
            return carry

        lax.fori_loop(0, H // 256, part, 0)

    def activate():
        def part(n, carry):
            cols = span(n, 128)
            pre, mul = pg[:, cols], pu[:, cols]
            sigma = jax.nn.sigmoid(pre)
            act = pre * sigma
            ht[cols, :] = jnp.transpose(act * mul).astype(BF16)
            pg[:, cols] = act
            pu[:, cols] = mul * sigma * (1.0 + pre * (1.0 - sigma))
            return carry

        lax.fori_loop(0, H // 128, part, 0)

    def backward(q):
        def part(n, carry):
            cols = span(n, 256)
            dh[:, cols] += dot(chunk_of(rows, q), wd[cols, span(q - NQ, C)], ((1,), (1,)))
            return carry

        lax.fori_loop(0, H // 256, part, 0)

    lefts, firsts = (ht, dgt, dut), (NQ, 0, 0)

    def shares(w, g):
        def part(n, carry):
            q = g * (GC // C) + n
            got = dot(lefts[w][...], chunk_of(rows, firsts[w] + q))
            pw[w * NG + g, :, :, :, span(n, C)] = got.astype(BF16).reshape(4, 2, HZ, C)
            return carry

        lax.fori_loop(0, GC // C, part, 0)

    def ring(u, src, dst, recv, i):
        copy(src, dst, ys_sem.at[0], recv, y_down if i else y_up).start()

    def send_far(u):
        for i in range(2):
            ring(u, pw.at[u, y2, i], ra.at[u, i], ya_sem.at[u, i], i)

    def send_near(u):
        for i in range(2):
            ring(u, pw.at[u, y3 if i else y1, 1 - i], rb.at[u, i, 1 - i], yb_sem.at[u], i)

    def relay(u):
        for i in range(2):
            landed(ra.at[u, i], ya_sem.at[u, i])
            at = y3 if i else y1
            pw[u, at, i] = (pw[u, at, i].astype(F32) + ra[u, i].astype(F32)).astype(BF16)
            ring(u, pw.at[u, at, i], rb.at[u, i, i], yb_sem.at[u], i)

    def mate_copy(u):
        return copy(pw.at[u, y, 1 - zl], given.at[u], ms_sem.at[0], mr_sem.at[u], mate)

    def ring_sum(u, half):
        return (pw[u, y, half].astype(F32) + rb[u, 0, half].astype(F32)
                + rb[u, 1, half].astype(F32))

    def settle(u):
        landed(rb.at[u], yb_sem.at[u])
        pw[u, y, 1 - zl] = ring_sum(u, 1 - zl).astype(BF16)
        mate_copy(u).start()

    def finish(w, g):
        u = w * NG + g
        landed(given.at[u], mr_sem.at[u])
        total = ring_sum(u, zl) + given[u].astype(F32)
        (down_out, gate_out, up_out)[w][:, span(g, GC)] = total

    def stage(s, carry):
        @pl.when(s + AHEAD < 2 * NQ)
        def _():
            send_own(s + AHEAD)

        @pl.when(s < 2 * NQ)
        def _():
            landed(blk.at[s, 2], zr_sem.at[s, 1])
            block_copy(s, 2).start()
            landed(blk.at[s, 1], zr_sem.at[s, 0])

        @pl.when(s == 1)
        def _():
            build()

        @pl.when((s >= 1) & (s < 2 * NQ + 1))
        def _():
            landed(blk.at[s - 1, 3], zr_sem.at[s - 1, 2])
            pick(s - 1)

        @pl.when(s == 1)
        def _():
            flip()

        @pl.when(s == 3)
        def _():
            for load in wloads:
                load.wait()

        @pl.when(s >= 3)
        def _():
            q = s - 3
            landed(rows.at[q, pl.ds(0, NE - 1)], xr_sem.at[q])

            @pl.when(q < NQ)
            def _():
                forward(q)

            @pl.when(q == NQ - 1)
            def _():
                activate()

            @pl.when(q >= NQ)
            def _():
                backward(q)

            @pl.when((q > NQ) & (lax.rem(q, GC // C) == GC // C - 1))
            def _():
                g = lax.div(q - NQ, GC // C)
                shares(0, g)
                send_far(g)
                send_near(g)

                @pl.when(g >= 1)
                def _():
                    relay(g - 1)

                @pl.when(g >= 2)
                def _():
                    settle(g - 2)

        return carry

    lax.fori_loop(0, 2 * NQ + 3, stage, 0)

    def derive(n, carry):
        cols = span(n, 128)
        grad = dh[:, cols]
        d_up = grad * pg[:, cols]
        d_gate = grad * pu[:, cols]
        du[:, cols] = d_up.astype(BF16)
        dg[:, cols] = d_gate.astype(BF16)
        dut[cols, :] = jnp.transpose(d_up).astype(BF16)
        dgt[cols, :] = jnp.transpose(d_gate).astype(BF16)
        return carry

    lax.fori_loop(0, H // 128, derive, 0)

    landed(snd.at[:, pl.ds(0, NE - 1)], xs_sem.at[0])
    landed(blk.at[:, pl.ds(0, 3)], zs_sem.at[0])
    landed(info.at[pl.ds(0, 3)], is_sem.at[0])

    def back(q):
        at = span(q, C)
        got = dot(dg[...], wg[at, :], ((1,), (1,))) + dot(du[...], wu[at, :], ((1,), (1,)))
        snd[q] = got.astype(BF16).reshape(NE, PAD, C)
        spread(snd.at[q], brow.at[q], bs_sem.at[0], br_sem.at[q])
        brow[q, xc] = snd[q, xc]

    for w in (1, 2):
        def both(g, carry):
            shares(w, g)
            send_far(w * NG + g)
            back((w - 1) * NG + g)
            return carry

        lax.fori_loop(0, NG, both, 0)

    def near(u, carry):
        send_near(u)
        return carry

    lax.fori_loop(NG, NU, near, 0)

    def t_copy(q, b):
        at = 2 if b == 3 else zl
        return copy(blk.at[q, b], trow.at[q, at], ts_sem.at[0], tr_sem.at[q, at],
                    prev_other if b == 2 else prev_same)

    def own_sum(q):
        return pl.ds(pl.multiple_of(lax.rem(q, 4) * TOK, TOK), TOK), span(lax.div(q, 4), C)

    def combine(q):
        landed(brow.at[q, pl.ds(0, NE - 1)], br_sem.at[q])
        got = dot(selt[...], chunk_of(brow, q)).reshape(NB, TOK, C)
        blk[q, pl.ds(1, 3)] = got[1:].astype(BF16)
        t_copy(q, 3).start()
        t_copy(q, 1).start()
        pg[own_sum(q)] = got[0]

    def pass_on(q):
        landed(trow.at[q, 2], tr_sem.at[q, 2])
        blk[q, 2] = (blk[q, 2].astype(F32) + trow[q, 2].astype(F32)).astype(BF16)
        t_copy(q, 2).start()

    relay(NG - 1)
    settle(NG - 2)

    def return_step(q, carry):
        @pl.when(q < NQ)
        def _():
            combine(q)
            relay(NG + q)

        @pl.when(q >= 1)
        def _():
            pass_on(q - 1)

        return carry

    lax.fori_loop(0, NQ + 1, return_step, 0)
    settle(NG - 1)
    for g in range(NG):
        finish(0, g)

    def finish_tokens(q):
        landed(trow.at[q, 0], tr_sem.at[q, 0])
        landed(trow.at[q, 1], tr_sem.at[q, 1])
        total = pg[own_sum(q)] + trow[q, 0].astype(F32) + trow[q, 1].astype(F32)
        tg_out[:, span(q, C)] = total.astype(BF16)

    for w in (1, 2):
        def last(g, carry):
            settle(w * NG + g)
            finish_tokens((w - 1) * NG + g)

            @pl.when(g >= 1)
            def _():
                finish(w, g - 1)

            return carry

        lax.fori_loop(0, NG, last, 0)
        finish(w, NG - 1)

    landed(pw.at[:, pl.ds(0, 3)], ys_sem.at[0])
    landed(pw.at[:, 0, 0], ms_sem.at[0])
    landed(snd.at[pl.ds(0, NQ), pl.ds(0, NE - 1)], bs_sem.at[0])
    landed(blk.at[pl.ds(0, NQ), pl.ds(1, 3)], ts_sem.at[0])


PIECES = 2


def hand_on_kernel(*refs):
    ins, outs, held, sem_in, sem_out = refs[0:4], refs[4:8], refs[8:12], refs[12], refs[13]
    loads, stores = [], []
    for i in range(4):
        part = ins[i].shape[0] // PIECES
        for n in range(PIECES):
            at = pl.ds(n * part, part)
            loads.append(pltpu.make_async_copy(ins[i].at[at], held[i].at[at], sem_in.at[i, n]))
            stores.append(pltpu.make_async_copy(held[i].at[at], outs[i].at[at], sem_out.at[i, n]))
    for c in loads:
        c.start()
    for load, store in zip(loads, stores):
        load.wait()
        store.start()
    for c in stores:
        c.wait()


def hand_on(results):
    hbm = pl.BlockSpec(memory_space=pl.ANY)
    return pl.pallas_call(
        hand_on_kernel,
        out_shape=tuple(jax.ShapeDtypeStruct(r.shape, r.dtype) for r in results),
        in_specs=[hbm] * 4,
        out_specs=(hbm,) * 4,
        scratch_shapes=[pltpu.VMEM(r.shape, r.dtype) for r in results]
        + [pltpu.SemaphoreType.DMA((4, PIECES))] * 2,
        cost_estimate=pl.CostEstimate(
            flops=0, bytes_accessed=6 * 1024 * 1024, transcendentals=0),
    )(*results)


def body(tokens, cotangent, routes, gates, w_gate, w_up, w_down):
    hbm = pl.BlockSpec(memory_space=pl.ANY)
    vmem = pl.BlockSpec(memory_space=pltpu.VMEM)
    V, S = pltpu.VMEM, pltpu.SemaphoreType.DMA
    results = pl.pallas_call(
        kernel,
        out_shape=(
            jax.ShapeDtypeStruct((TOK, D), BF16),
            jax.ShapeDtypeStruct((HZ, D), F32),
            jax.ShapeDtypeStruct((HZ, D), F32),
            jax.ShapeDtypeStruct((HZ, D), F32),
        ),
        in_specs=[vmem, vmem, hbm, hbm, hbm, hbm, hbm],
        out_specs=(vmem, vmem, vmem, vmem),
        scratch_shapes=[
            V((NB, 2 * TOP, TOK), F32),
            V((2 * NQ, NB, TOK, C), BF16),
            V((ROWS, NB * TOK), BF16), V((NB * TOK, ROWS), BF16),
            V((ROWS, 128), F32),
            V((2 * NQ, NE, PAD, C), BF16),
            V((2 * NQ, NE, PAD, C), BF16),
            V((D, H), BF16), V((D, H), BF16), V((H, D), BF16),
            V((ROWS, H), F32), V((ROWS, H), F32), V((ROWS, H), F32),
            V((H, ROWS), BF16), V((H, ROWS), BF16), V((H, ROWS), BF16),
            V((ROWS, H), BF16), V((ROWS, H), BF16),
            V((NQ, NE, PAD, C), BF16),
            V((NQ, 3, TOK, C), BF16),
            V((NU, 4, 2, HZ, GC), BF16),
            V((NU, 2, HZ, GC), BF16),
            V((NU, 2, 2, HZ, GC), BF16),
            V((NU, HZ, GC), BF16),
            S((2 * NQ,)), S((3,)), S((1,)), S((3,)),
            S((1,)), S((2 * NQ, 3)), S((1,)), S((2 * NQ,)),
            S((1,)), S((NQ,)), S((1,)), S((NQ, 3)),
            S((1,)), S((NU, 2)), S((NU,)), S((1,)), S((NU,)),
        ],
        compiler_params=pltpu.CompilerParams(
            collective_id=0, has_side_effects=True, vmem_limit_bytes=62 * 1024 * 1024),
        cost_estimate=pl.CostEstimate(
            flops=8 * 2 * ROWS * D * H, bytes_accessed=16 * 1024 * 1024, transcendentals=ROWS * H),
    )(routes.T, gates.T, tokens, cotangent, w_gate, w_up, w_down)
    token_grad, down, gate, up = hand_on(results)
    return token_grad, gate.T[None], up.T[None], down[None]


def solution(mesh):
    rows = P(("dp", "expert"), None)
    return jax.shard_map(
        body,
        mesh=mesh,
        in_specs=(rows, rows, rows, rows) + (P("expert", None, None),) * 3,
        out_specs=(rows, P("expert", None, "dp"), P("expert", None, "dp"), P("expert", "dp", None)),
        check_vma=False,
    )
```

time: 206 us -> 179 us (0.87); the launches traced: 206 us -> 176 us
  Pallas kernels: 197 us -> 175 us
  local copies, waits for them, and re-layouts: 5.83 us -> 0 us
    pallas_call x1, Pallas kernels: 197 us -> 173 us  [body(): pl.pallas_call(kernel, out_shape=(jax.ShapeDtypeStruct((TOK, D), BF16), j...]
    unnamed x8 -> x0, local copies, waits for them, and re-layouts: 5.83 us -> none
    pallas_call x0 -> x1, Pallas kernels: none -> 2.69 us  [hand_on(): pl.pallas_call(hand_on_kernel, out_shape=tuple((jax.ShapeDtypeStruct(r.sh...]
where the time goes in v2:
time: 179 us; the launch traced here: 176 us
  Pallas kernels  175 us (98%)
    pallas_call x1, Pallas kernels, body(): pl.pallas_call(kernel, out_shape=(jax.ShapeDtypeStruct((TOK, D), BF16), j...  173 us

profile of v2, /device:TPU:1, one launch (start us, length us, event | category | flops | bytes accessed | tf_op | source)
XLA Modules:
  0.0 176.0 jit_solution(3711449361482158395)
XLA Ops:
  0.6 172.6 %shard_map.102 = (bf16[128,2048]{1,0:T(8,128)(2,1)}, f32[96,2048]{1,0:T(8,128)}, f32[96,2048]{1,0:T(8,128)}, f32[96,2048]{1,0:T(8,128)}) custom-call(s32[4,128]{1,0:T(4,128)} %bitcast.12, f32[4,128]{1,0:T(4,128)} %bitcast.13, bf16[128,2048]{1,0:T(8,128)(2,1)} %tok_in.1, bf16[128,2048]{1,0:T(8,128)(2,1)} %cot_in.1, bf16[1,2048,768]{2,1,0:T(8,128)(2,1)} %wg_in.1, ...), custom_call_target="tpu_custom_call" | custom-call | flops 16106127360 | bytes 16777216 | tf_op jit(solution)/shard_map/pallas_call | solution.py:462
  173.3 2.7 %shard_map.103 = (bf16[128,2048]{1,0:T(8,128)(2,1)}, f32[96,2048]{1,0:T(8,128)}, f32[96,2048]{1,0:T(8,128)}, f32[96,2048]{1,0:T(8,128)}) custom-call(bf16[128,2048]{1,0:T(8,128)(2,1)} %get-tuple-element.12.refs_0_, f32[96,2048]{1,0:T(8,128)} %get-tuple-element.13.refs_1_, f32[96,2048]{1,0:T(8,128)} %get-tuple-element.14.refs_2_, ...), custom_call_target="tpu_custom_call" | custom-call | bytes 6291456 | tf_op jit(solution)/shard_map/pallas_call | solution.py:446

commit v3 on v2

--- a/solution.py
+++ b/solution.py
@@ -20,8 +20,10 @@
 ROWS = NE * PAD
 NQ = 8
 C = D // NQ
-AHEAD = 4
-NG = 4
+AHEAD = 2
+WINDOW = 2
+LAG = 1
+NG = 8
 GC = D // NG
 NU = 3 * NG
 HY = H // 4
@@ -34,7 +36,7 @@
 
 def kernel(
     routes_in, gates_in, tok_in, cot_in, wg_in, wu_in, wd_in,
-    tg_out, down_out, gate_out, up_out,
+    tg_out, grads_out,
     info, blk, sel, selt, sgate, snd, rows, wg, wu, wd, pg, pu, dh,
     ht, dgt, dut, dg, du, brow, trow, pw, ra, rb, given,
     in_sem, w_sem, is_sem, ir_sem, zs_sem, zr_sem, xs_sem, xr_sem,
@@ -243,11 +245,11 @@
         pw[u, y, 1 - zl] = ring_sum(u, 1 - zl).astype(BF16)
         mate_copy(u).start()
 
-    def finish(w, g):
-        u = w * NG + g
+    def finish(u):
+        w, g = lax.div(u, NG), lax.rem(u, NG)
         landed(given.at[u], mr_sem.at[u])
         total = ring_sum(u, zl) + given[u].astype(F32)
-        (down_out, gate_out, up_out)[w][:, span(g, GC)] = total
+        grads_out[w, :, span(g, GC)] = total
 
     def stage(s, carry):
         @pl.when(s + AHEAD < 2 * NQ)
@@ -264,10 +266,10 @@
         def _():
             build()
 
-        @pl.when((s >= 1) & (s < 2 * NQ + 1))
-        def _():
-            landed(blk.at[s - 1, 3], zr_sem.at[s - 1, 2])
-            pick(s - 1)
+        @pl.when((s >= LAG) & (s < 2 * NQ + LAG))
+        def _():
+            landed(blk.at[s - LAG, 3], zr_sem.at[s - LAG, 2])
+            pick(s - LAG)
 
         @pl.when(s == 1)
         def _():
@@ -278,9 +280,9 @@
             for load in wloads:
                 load.wait()
 
-        @pl.when(s >= 3)
-        def _():
-            q = s - 3
+        @pl.when(s >= LAG + 2)
+        def _():
+            q = s - LAG - 2
             landed(rows.at[q, pl.ds(0, NE - 1)], xr_sem.at[q])
 
             @pl.when(q < NQ)
@@ -295,9 +297,9 @@
             def _():
                 backward(q)
 
-            @pl.when((q > NQ) & (lax.rem(q, GC // C) == GC // C - 1))
+            @pl.when(q >= NQ)
             def _():
-                g = lax.div(q - NQ, GC // C)
+                g = q - NQ
                 shares(0, g)
                 send_far(g)
                 send_near(g)
@@ -312,7 +314,7 @@
 
         return carry
 
-    lax.fori_loop(0, 2 * NQ + 3, stage, 0)
+    lax.fori_loop(0, 2 * NQ + LAG + 2, stage, 0)
 
     def derive(n, carry):
         cols = span(n, 128)
@@ -342,16 +344,14 @@
         def both(g, carry):
             shares(w, g)
             send_far(w * NG + g)
-            back((w - 1) * NG + g)
+
+            @pl.when(lax.rem(g, 2) == 0)
+            def _():
+                back((w - 1) * (NG // 2) + lax.div(g, 2))
+
             return carry
 
         lax.fori_loop(0, NG, both, 0)
-
-    def near(u, carry):
-        send_near(u)
-        return carry
-
-    lax.fori_loop(NG, NU, near, 0)
 
     def t_copy(q, b):
         at = 2 if b == 3 else zl
@@ -374,45 +374,49 @@
         blk[q, 2] = (blk[q, 2].astype(F32) + trow[q, 2].astype(F32)).astype(BF16)
         t_copy(q, 2).start()
 
-    relay(NG - 1)
-    settle(NG - 2)
-
-    def return_step(q, carry):
-        @pl.when(q < NQ)
-        def _():
-            combine(q)
-            relay(NG + q)
-
-        @pl.when(q >= 1)
-        def _():
-            pass_on(q - 1)
-
-        return carry
-
-    lax.fori_loop(0, NQ + 1, return_step, 0)
-    settle(NG - 1)
-    for g in range(NG):
-        finish(0, g)
-
     def finish_tokens(q):
         landed(trow.at[q, 0], tr_sem.at[q, 0])
         landed(trow.at[q, 1], tr_sem.at[q, 1])
         total = pg[own_sum(q)] + trow[q, 0].astype(F32) + trow[q, 1].astype(F32)
         tg_out[:, span(q, C)] = total.astype(BF16)
 
-    for w in (1, 2):
-        def last(g, carry):
-            settle(w * NG + g)
-            finish_tokens((w - 1) * NG + g)
-
-            @pl.when(g >= 1)
-            def _():
-                finish(w, g - 1)
-
-            return carry
-
-        lax.fori_loop(0, NG, last, 0)
-        finish(w, NG - 1)
+    relay(NG - 1)
+
+    def return_step(i, carry):
+        @pl.when(i < NQ)
+        def _():
+            for n in range(2):
+                send_near(NG + 2 * i + n)
+                relay(NG + 2 * i + n)
+            combine(i)
+
+        @pl.when(i == 0)
+        def _():
+            settle(NG - 2)
+            settle(NG - 1)
+
+        @pl.when((i >= 1) & (i < NQ + 1))
+        def _():
+            pass_on(i - 1)
+            finish(i - 1)
+
+        @pl.when(i >= WINDOW)
+        def _():
+            for n in range(2):
+                settle(NG + 2 * (i - WINDOW) + n)
+
+        @pl.when(i >= WINDOW + 1)
+        def _():
+            finish_tokens(i - WINDOW - 1)
+            for n in range(2):
+                finish(NG + 2 * (i - WINDOW - 1) + n)
+
+        return carry
+
+    lax.fori_loop(0, NQ + WINDOW, return_step, 0)
+    finish_tokens(NQ - 1)
+    for n in range(2):
+        finish(NU - 2 + n)
 
     landed(pw.at[:, pl.ds(0, 3)], ys_sem.at[0])
     landed(pw.at[:, 0, 0], ms_sem.at[0])
@@ -424,14 +428,17 @@
 
 
 def hand_on_kernel(*refs):
-    ins, outs, held, sem_in, sem_out = refs[0:4], refs[4:8], refs[8:12], refs[12], refs[13]
+    token_in, grads_in, outs = refs[0], refs[1], refs[2:6]
+    token_held, grads_held, sem_in, sem_out = refs[6:10]
     loads, stores = [], []
     for i in range(4):
-        part = ins[i].shape[0] // PIECES
+        src = grads_in.at[i - 1] if i else token_in
+        mid = grads_held.at[i - 1] if i else token_held
+        part = src.shape[0] // PIECES
         for n in range(PIECES):
             at = pl.ds(n * part, part)
-            loads.append(pltpu.make_async_copy(ins[i].at[at], held[i].at[at], sem_in.at[i, n]))
-            stores.append(pltpu.make_async_copy(held[i].at[at], outs[i].at[at], sem_out.at[i, n]))
+            loads.append(pltpu.make_async_copy(src.at[at], mid.at[at], sem_in.at[i, n]))
+            stores.append(pltpu.make_async_copy(mid.at[at], outs[i].at[at], sem_out.at[i, n]))
     for c in loads:
         c.start()
     for load, store in zip(loads, stores):
@@ -445,8 +452,9 @@
     hbm = pl.BlockSpec(memory_space=pl.ANY)
     return pl.pallas_call(
         hand_on_kernel,
-        out_shape=tuple(jax.ShapeDtypeStruct(r.shape, r.dtype) for r in results),
-        in_specs=[hbm] * 4,
+        out_shape=(jax.ShapeDtypeStruct((TOK, D), BF16),)
+        + (jax.ShapeDtypeStruct((HZ, D), F32),) * 3,
+        in_specs=[hbm] * 2,
         out_specs=(hbm,) * 4,
         scratch_shapes=[pltpu.VMEM(r.shape, r.dtype) for r in results]
         + [pltpu.SemaphoreType.DMA((4, PIECES))] * 2,
@@ -463,12 +471,10 @@
         kernel,
         out_shape=(
             jax.ShapeDtypeStruct((TOK, D), BF16),
-            jax.ShapeDtypeStruct((HZ, D), F32),
-            jax.ShapeDtypeStruct((HZ, D), F32),
-            jax.ShapeDtypeStruct((HZ, D), F32),
+            jax.ShapeDtypeStruct((3, HZ, D), F32),
         ),
         in_specs=[vmem, vmem, hbm, hbm, hbm, hbm, hbm],
-        out_specs=(vmem, vmem, vmem, vmem),
+        out_specs=(vmem, vmem),
         scratch_shapes=[
             V((NB, 2 * TOP, TOK), F32),
             V((2 * NQ, NB, TOK, C), BF16),

time: 179 us -> 166 us (0.927); the launches traced: 176 us -> 166 us
  Pallas kernels: 175 us -> 166 us
    pallas_call x1, Pallas kernels: 173 us -> 163 us  [body(): pl.pallas_call(kernel, out_shape=(jax.ShapeDtypeStruct((TOK, D), BF16), j...]
where the time goes in v3:
time: 166 us
  Pallas kernels  166 us (100%)
    pallas_call x1, Pallas kernels, body(): pl.pallas_call(kernel, out_shape=(jax.ShapeDtypeStruct((TOK, D), BF16), j...  163 us

profile of v3, /device:TPU:1, one launch (start us, length us, event | category | flops | bytes accessed | tf_op | source)
XLA Modules:
  0.0 166.2 jit_solution(11502643707355669889)
XLA Ops:
  0.6 162.8 %shard_map.102 = (bf16[128,2048]{1,0:T(8,128)(2,1)}, f32[3,96,2048]{2,1,0:T(8,128)}) custom-call(s32[4,128]{1,0:T(4,128)} %bitcast.12, f32[4,128]{1,0:T(4,128)} %bitcast.13, bf16[128,2048]{1,0:T(8,128)(2,1)} %tok_in.1, bf16[128,2048]{1,0:T(8,128)(2,1)} %cot_in.1, bf16[1,2048,768]{2,1,0:T(8,128)(2,1)} %wg_in.1, bf16[1,2048,768]{2,1,0:T(8,128)(2,1)} %wu_in.1, ...), custom_call_target="tpu_custom_call" | custom-call | flops 16106127360 | bytes 16777216 | tf_op jit(solution)/shard_map/pallas_call | solution.py:470
  163.5 2.7 %shard_map.103 = (bf16[128,2048]{1,0:T(8,128)(2,1)}, f32[96,2048]{1,0:T(8,128)}, f32[96,2048]{1,0:T(8,128)}, f32[96,2048]{1,0:T(8,128)}) custom-call(bf16[128,2048]{1,0:T(8,128)(2,1)} %get-tuple-element.10.refs_0_, f32[3,96,2048]{2,1,0:T(8,128)} %get-tuple-element.11.refs_1_), custom_call_target="tpu_custom_call" | custom-call | bytes 6291456 | tf_op jit(solution)/shard_map/pallas_call | solution.py:453

commit v4 on v3

--- a/solution.py
+++ b/solution.py
@@ -21,7 +21,8 @@
 NQ = 8
 C = D // NQ
 AHEAD = 2
-WINDOW = 2
+WINDOW = 6
+COMBINE = 9
 LAG = 1
 NG = 8
 GC = D // NG
@@ -316,18 +317,21 @@
 
     lax.fori_loop(0, 2 * NQ + LAG + 2, stage, 0)
 
-    def derive(n, carry):
-        cols = span(n, 128)
-        grad = dh[:, cols]
-        d_up = grad * pg[:, cols]
-        d_gate = grad * pu[:, cols]
-        du[:, cols] = d_up.astype(BF16)
-        dg[:, cols] = d_gate.astype(BF16)
-        dut[cols, :] = jnp.transpose(d_up).astype(BF16)
-        dgt[cols, :] = jnp.transpose(d_gate).astype(BF16)
-        return carry
-
-    lax.fori_loop(0, H // 128, derive, 0)
+    def derive(factor, flat, turned):
+        def part(n, carry):
+            cols = span(n, 128)
+            grad = dh[:, cols] * factor[:, cols]
+            flat[:, cols] = grad.astype(BF16)
+            turned[cols, :] = jnp.transpose(grad).astype(BF16)
+            return carry
+
+        lax.fori_loop(0, H // 128, part, 0)
+
+    derive(pu, dg, dgt)
+    for g in range(2):
+        shares(1, g)
+        send_far(NG + g)
+    derive(pg, du, dut)
 
     landed(snd.at[:, pl.ds(0, NE - 1)], xs_sem.at[0])
     landed(blk.at[:, pl.ds(0, 3)], zs_sem.at[0])
@@ -339,19 +343,6 @@
         snd[q] = got.astype(BF16).reshape(NE, PAD, C)
         spread(snd.at[q], brow.at[q], bs_sem.at[0], br_sem.at[q])
         brow[q, xc] = snd[q, xc]
-
-    for w in (1, 2):
-        def both(g, carry):
-            shares(w, g)
-            send_far(w * NG + g)
-
-            @pl.when(lax.rem(g, 2) == 0)
-            def _():
-                back((w - 1) * (NG // 2) + lax.div(g, 2))
-
-            return carry
-
-        lax.fori_loop(0, NG, both, 0)
 
     def t_copy(q, b):
         at = 2 if b == 3 else zl
@@ -380,40 +371,68 @@
         total = pg[own_sum(q)] + trow[q, 0].astype(F32) + trow[q, 1].astype(F32)
         tg_out[:, span(q, C)] = total.astype(BF16)
 
+    def push(u):
+        send_near(u)
+        relay(u)
+
+    def mixed_step(w, g, carry):
+        it = (w - 1) * NG + g
+        shares(w, g)
+        send_far(w * NG + g)
+
+        @pl.when(it >= 2 * NG - WINDOW)
+        def _():
+            push(NG + it - (2 * NG - WINDOW))
+
+        @pl.when(it < NQ + 2)
+        def _():
+            back(it - 2)
+
+        @pl.when((it >= COMBINE) & (lax.rem(it - COMBINE, 2) == 0))
+        def _():
+            combine(lax.div(it - COMBINE, 2))
+
+        @pl.when((it >= COMBINE + 4) & (lax.rem(it - COMBINE, 2) == 0))
+        def _():
+            pass_on(lax.div(it - COMBINE - 4, 2))
+
+        return carry
+
+    lax.fori_loop(2, NG, lambda g, c: mixed_step(1, g, c), 0)
     relay(NG - 1)
+    settle(NG - 2)
+    lax.fori_loop(0, NG, lambda g, c: mixed_step(2, g, c), 0)
+    settle(NG - 1)
+    summed, passed = (2 * NG + 1 - COMBINE) // 2, (2 * NG - 3 - COMBINE) // 2
 
     def return_step(i, carry):
-        @pl.when(i < NQ)
+        @pl.when(2 * i < 2 * NG - WINDOW)
         def _():
             for n in range(2):
-                send_near(NG + 2 * i + n)
-                relay(NG + 2 * i + n)
-            combine(i)
-
-        @pl.when(i == 0)
-        def _():
-            settle(NG - 2)
-            settle(NG - 1)
-
-        @pl.when((i >= 1) & (i < NQ + 1))
-        def _():
-            pass_on(i - 1)
-            finish(i - 1)
-
-        @pl.when(i >= WINDOW)
+                push(NG + WINDOW + 2 * i + n)
+
+        @pl.when(i < NQ - summed)
+        def _():
+            combine(summed + i)
+
+        @pl.when(i < NQ - passed)
+        def _():
+            pass_on(passed + i)
+
+        for n in range(2):
+            settle(NG + 2 * i + n)
+
+        finish(i)
+
+        @pl.when(i >= 1)
         def _():
             for n in range(2):
-                settle(NG + 2 * (i - WINDOW) + n)
-
-        @pl.when(i >= WINDOW + 1)
-        def _():
-            finish_tokens(i - WINDOW - 1)
-            for n in range(2):
-                finish(NG + 2 * (i - WINDOW - 1) + n)
+                finish(NG + 2 * (i - 1) + n)
+            finish_tokens(i - 1)
 
         return carry
 
-    lax.fori_loop(0, NQ + WINDOW, return_step, 0)
+    lax.fori_loop(0, NG, return_step, 0)
     finish_tokens(NQ - 1)
     for n in range(2):
         finish(NU - 2 + n)

time: 166 us -> 164 us (0.988)
  Pallas kernels: 166 us -> 163 us
    pallas_call x1, Pallas kernels: 163 us -> 161 us  [body(): pl.pallas_call(kernel, out_shape=(jax.ShapeDtypeStruct((TOK, D), BF16), j...]
where the time goes in v4:
time: 164 us
  Pallas kernels  163 us (99%)
    pallas_call x1, Pallas kernels, body(): pl.pallas_call(kernel, out_shape=(jax.ShapeDtypeStruct((TOK, D), BF16), j...  161 us

profile of v4, /device:TPU:1, one launch (start us, length us, event | category | flops | bytes accessed | tf_op | source)
XLA Modules:
  0.0 163.8 jit_solution(17207184862094278975)
XLA Ops:
  0.6 160.5 %shard_map.102 = (bf16[128,2048]{1,0:T(8,128)(2,1)}, f32[3,96,2048]{2,1,0:T(8,128)}) custom-call(s32[4,128]{1,0:T(4,128)} %bitcast.12, f32[4,128]{1,0:T(4,128)} %bitcast.13, bf16[128,2048]{1,0:T(8,128)(2,1)} %tok_in.1, bf16[128,2048]{1,0:T(8,128)(2,1)} %cot_in.1, bf16[1,2048,768]{2,1,0:T(8,128)(2,1)} %wg_in.1, bf16[1,2048,768]{2,1,0:T(8,128)(2,1)} %wu_in.1, ...), custom_call_target="tpu_custom_call" | custom-call | flops 16106127360 | bytes 16777216 | tf_op jit(solution)/shard_map/pallas_call | solution.py:489
  161.1 2.7 %shard_map.103 = (bf16[128,2048]{1,0:T(8,128)(2,1)}, f32[96,2048]{1,0:T(8,128)}, f32[96,2048]{1,0:T(8,128)}, f32[96,2048]{1,0:T(8,128)}) custom-call(bf16[128,2048]{1,0:T(8,128)(2,1)} %get-tuple-element.10.refs_0_, f32[3,96,2048]{2,1,0:T(8,128)} %get-tuple-element.11.refs_1_), custom_call_target="tpu_custom_call" | custom-call | bytes 6291456 | tf_op jit(solution)/shard_map/pallas_call | solution.py:472
